TPU v7x, 32 devices: a whole 2x2x4 slice. The times are simulated.
32 devices in a mesh: dp: 8 (over y, x, core), tensor: 4 (over z).
Axes of the slice: x: 2, y: 2, z: 4, core: 2. Of those that a mesh axis runs over, the one named last changes fastest.
Arguments:
- hidden: bfloat16 [2048, 5120], P('dp', 'tensor'), may hold values from -6 to 6
- norm_gain: float32 [5120], replicated, may hold values from 0.1 to 1.9
- w_query: bfloat16 [5120, 8192], P(None, 'tensor'), may hold values from -0.078125 to 0.078125
- key_projection_weight: bfloat16 [5120, 1024], P(None, 'tensor'), may hold values from -0.078125 to 0.078125
- value_projection_weight: bfloat16 [5120, 1024], P(None, 'tensor'), may hold values from -0.078125 to 0.078125
- query_gain: float32 [128], replicated, may hold values from 1 to 4
- key_gain: float32 [128], replicated, may hold values from 0.5 to 2
- kv_pool: bfloat16 [3072, 8, 2, 16, 128], P(('dp', 'tensor')), may hold values from -102 to 102
- page_owner: int32 [8, 256], replicated, may hold values from 0 to 31, as said below
- page_slot: int32 [8, 256], replicated, may hold values from 0 to 95, as said below
- prefix_len: int32 [8], P('dp'), may hold values from 512 to 4096, as said below
- new_owner: int32 [8, 16, 1], P('dp'), may hold values from 0 to 7; in each aligned block of 16 rows (0 to 15, 16 to 31, ..., all dimensions but the last counted through in order) at most 2 rows name the same one
Outputs:
- attn_out: bfloat16 [2048, 8192], P('dp', 'tensor')
- fresh_page_store: bfloat16 [128, 8, 2, 16, 128], P('dp', 'tensor')
Inputs may be any that keep to these rules, and one draw needn't show every extreme that they name: `page_owner`: for each request, no device owns more than 12 of its pages, and some device owns exactly 12. `page_slot`: the pages that one device owns sit in distinct slots. `prefix_len`: one request has the most cached tokens and one the least. `new_owner`: no dp index stores more than 2 new pages of one request.
All inputs are finite; a program needn't handle non-finite values.
Results may differ from a plain program's by a relative error of at most 0.006.
The roundings to bfloat16 on the way count: a program that leaves them out, or rounds other values in their place, can miss the bound.
Values may be sent and summed in bfloat16 or wider, within the bound.
A program may use at most 128 MiB of HBM per device.

v0:
```python
import math

import jax
import jax.numpy as jnp
from jax import lax
from jax.sharding import PartitionSpec as P

HEAD_SIZE = 128
PAGE_TOKENS = 16
SPAN = 256
NCAP = 2
MOST_PAGES = 256


EPS = 1e-06
THETA = 1000000.0
NEG = -1e30


def rms_rows(values, gain):
    mean_square = jnp.mean(values * values, axis=-1, keepdims=True)
    return values * lax.rsqrt(mean_square + EPS) * gain


def rotate(values, positions):
    half_width = values.shape[-1] // 2
    exponent = jnp.arange(half_width, dtype=jnp.float32) * (-2.0 / values.shape[-1])
    freqs = jnp.power(jnp.float32(THETA), exponent)
    angles = positions.astype(jnp.float32)[:, None] * freqs[None, :]
    cosine = jnp.cos(angles)[:, None, :]
    sine = jnp.sin(angles)[:, None, :]
    first_half = values[..., :half_width]
    second_half = values[..., half_width:]
    return jnp.concatenate(
        [first_half * cosine - second_half * sine, second_half * cosine + first_half * sine],
        axis=-1,
    )


def collect(matches, payload, capacity):
    ranks = jnp.cumsum(matches.astype(jnp.int32), axis=1) - 1
    places = jnp.arange(capacity, dtype=jnp.int32)
    landed = matches[:, :, None] & (ranks[:, :, None] == places[None, None, :])
    picked = jnp.sum(jnp.where(landed, payload[:, :, None], 0), axis=1)
    return (picked, jnp.any(landed, axis=1))


def shards(
    hidden,
    norm_gain,
    w_query,
    key_projection_weight,
    value_projection_weight,
    query_gain,
    key_gain,
    kv_pool,
    page_owner,
    page_slot,
    prefix_len,
    new_owner,
):
    data_ways = lax.axis_size("dp")
    tensor_ways = lax.axis_size("tensor")
    request = lax.axis_index("dp")
    slot_count = kv_pool.shape[0]
    capacity = slot_count // data_ways
    key_heads = key_projection_weight.shape[1] // HEAD_SIZE
    local_heads = w_query.shape[1] // HEAD_SIZE
    scale = 1.0 / math.sqrt(HEAD_SIZE)
    full_rows = lax.all_gather(hidden, "tensor", axis=1, tiled=True)
    normalized_rows = rms_rows(full_rows.astype(jnp.float32), norm_gain).astype(jnp.bfloat16)
    length = prefix_len[0]
    offsets = jnp.arange(SPAN, dtype=jnp.int32)
    positions = length + offsets
    query_flat = jnp.dot(normalized_rows, w_query, preferred_element_type=jnp.float32).reshape(
        SPAN, local_heads, HEAD_SIZE
    )
    flattened_keys = jnp.dot(
        normalized_rows, key_projection_weight, preferred_element_type=jnp.float32
    ).reshape(SPAN, key_heads, HEAD_SIZE)
    queries = rotate(rms_rows(query_flat, query_gain), positions).astype(jnp.bfloat16)
    new_keys = rotate(rms_rows(flattened_keys, key_gain), positions).astype(jnp.bfloat16)
    fresh_value_rows = (
        jnp.dot(normalized_rows, value_projection_weight, preferred_element_type=jnp.float32)
        .astype(jnp.bfloat16)
        .reshape(SPAN, key_heads, HEAD_SIZE)
    )
    page_count = SPAN // PAGE_TOKENS
    stacked_pages = jnp.stack([new_keys, fresh_value_rows], axis=2)
    fresh_pages = (
        stacked_pages.reshape(page_count, PAGE_TOKENS, key_heads, 2, HEAD_SIZE)
        .transpose(0, 2, 3, 1, 4)
        .reshape(page_count, key_heads * 2 * PAGE_TOKENS * HEAD_SIZE)
    )
    targets = new_owner[0, :, 0]
    page_index = jnp.arange(page_count, dtype=jnp.int32)
    earlier = page_index[None, :] < page_index[:, None]
    ranks = jnp.sum((targets[:, None] == targets[None, :]) & earlier, axis=1)
    slot_index = jnp.arange(data_ways * NCAP, dtype=jnp.int32)
    selector = ((targets * NCAP + ranks)[None, :] == slot_index[:, None]).astype(jnp.bfloat16)
    outgoing_pages = jnp.dot(selector, fresh_pages, preferred_element_type=jnp.float32).astype(
        jnp.bfloat16
    )
    outgoing_pages = outgoing_pages.reshape(data_ways * NCAP, key_heads, 2, PAGE_TOKENS, HEAD_SIZE)
    fresh_page_store = lax.all_to_all(outgoing_pages, "dp", split_axis=0, concat_axis=0, tiled=True)
    own_row = lax.dynamic_index_in_dim(page_owner, request, 0, keepdims=False)
    my_device = request * tensor_ways + lax.axis_index("tensor")
    picked, unused = collect(page_owner == my_device, page_slot, capacity)
    group_ids = jnp.arange(tensor_ways, dtype=jnp.int32)
    row_ids = picked[:, None, :] * tensor_ways + group_ids[None, :, None]
    flat_pool = kv_pool.reshape(slot_count * tensor_ways, key_heads * 2 * PAGE_TOKENS * HEAD_SIZE)
    outgoing = jnp.take(flat_pool, row_ids.reshape(-1), axis=0)
    arrived = lax.all_to_all(outgoing, ("dp", "tensor"), split_axis=0, concat_axis=0, tiled=True)
    sources = data_ways * tensor_ways
    received = arrived.reshape(sources, capacity, key_heads, 2, PAGE_TOKENS, HEAD_SIZE)
    source_match = own_row[None, :] == jnp.arange(sources, dtype=jnp.int32)[:, None]
    page_numbers = jnp.broadcast_to(
        jnp.arange(MOST_PAGES, dtype=jnp.int32)[None, :], (sources, MOST_PAGES)
    )
    page_of, present = collect(source_match, page_numbers, capacity)
    token_pos = (
        page_of[:, :, None] * PAGE_TOKENS + jnp.arange(PAGE_TOKENS, dtype=jnp.int32)[None, None, :]
    )
    live = (present[:, :, None] & (token_pos < length)).reshape(sources * capacity * PAGE_TOKENS)
    stored_key_rows = (
        received[:, :, :, 0]
        .transpose(2, 0, 1, 3, 4)
        .reshape(key_heads, sources * capacity * PAGE_TOKENS, HEAD_SIZE)
    )
    stored_value_rows = (
        received[:, :, :, 1]
        .transpose(2, 0, 1, 3, 4)
        .reshape(key_heads, sources * capacity * PAGE_TOKENS, HEAD_SIZE)
    )
    heads_per_group = local_heads // key_heads
    queries_by_head = queries.transpose(1, 0, 2)
    row_offsets = jnp.arange(2 * SPAN, dtype=jnp.int32) % SPAN
    causal = row_offsets[:, None] >= offsets[None, :]

    def pair_block(block):
        head_rows = lax.dynamic_slice_in_dim(queries_by_head, 2 * block, 2, 0).reshape(
            2 * SPAN, HEAD_SIZE
        )
        kv_index = 2 * block // heads_per_group
        prior_keys = lax.dynamic_index_in_dim(stored_key_rows, kv_index, 0, keepdims=False)
        prior_values = lax.dynamic_index_in_dim(stored_value_rows, kv_index, 0, keepdims=False)
        span_keys = lax.dynamic_index_in_dim(new_keys, kv_index, 1, keepdims=False)
        span_values = lax.dynamic_index_in_dim(fresh_value_rows, kv_index, 1, keepdims=False)
        prior = (
            jnp.einsum("qd,kd->qk", head_rows, prior_keys, preferred_element_type=jnp.float32)
            * scale
        )
        prior = jnp.where(live[None, :], prior, NEG)
        recent = (
            jnp.einsum("qd,kd->qk", head_rows, span_keys, preferred_element_type=jnp.float32)
            * scale
        )
        recent = jnp.where(causal, recent, NEG)
        peak = jnp.maximum(jnp.max(prior, axis=1), jnp.max(recent, axis=1))[:, None]
        prior_exp = jnp.exp(prior - peak)
        recent_exp = jnp.exp(recent - peak)
        total = jnp.sum(prior_exp, axis=1) + jnp.sum(recent_exp, axis=1)
        mixed = jnp.dot(
            prior_exp.astype(jnp.bfloat16), prior_values, preferred_element_type=jnp.float32
        )
        mixed = mixed + jnp.dot(
            recent_exp.astype(jnp.bfloat16), span_values, preferred_element_type=jnp.float32
        )
        return (mixed / total[:, None]).astype(jnp.bfloat16)

    blocks = lax.map(pair_block, jnp.arange(local_heads // 2, dtype=jnp.int32))
    attn_out = (
        blocks.reshape(local_heads, SPAN, HEAD_SIZE)
        .transpose(1, 0, 2)
        .reshape(SPAN, local_heads * HEAD_SIZE)
    )
    return (attn_out, fresh_page_store)


def solution(mesh):
    return jax.shard_map(
        shards,
        mesh=mesh,
        in_specs=(
            P("dp", "tensor"),
            P(),
            P(None, "tensor"),
            P(None, "tensor"),
            P(None, "tensor"),
            P(),
            P(),
            P(("dp", "tensor"), None, None, None, None),
            P(),
            P(),
            P("dp"),
            P("dp", None, None),
        ),
        out_specs=(P("dp", "tensor"), P("dp", "tensor", None, None, None)),
        check_vma=False,
    )
```

profile of v0, /device:TPU:7, one launch (start us, length us, event | category | flops | bytes accessed | tf_op | source)
XLA Modules:
  0.0 418.5 jit_solution(4888449600047418253)
XLA Ops:
  10.2 1.0 select_reduce_fusion.1
  11.4 10.5 %reshape.340 = bf16[384,8192]{1,0:T(8,128)(2,1)} reshape(bf16[96,8,2,16,128]{4,3,2,1,0:T(8,128)(2,1)} %param.21) | data formatting | bytes 12582912 | tf_op jit(solution)/shard_map/reshape | solution.py:111
  21.9 18.4 %gather_fusion = bf16[384,8192]{1,0:T(8,128)(2,1)} fusion(bf16[384,8192]{1,0:T(8,128)(2,1)} %reshape.340, s32[1024]{0:T(1024)S(1)} %pad_clamp_fusion), kind=kCustom, calls=%fused_computation | custom fusion | bytes 12584448 | tf_op jit(solution)/shard_map/jit(_take)/gather | solution.py:112
  40.4 8.6 %gather.7 = bf16[32,12,8192]{2,1,0:T(8,128)(2,1)} reshape(bf16[384,8192]{1,0:T(8,128)(2,1)} %gather_fusion) | data formatting | bytes 12582912 | tf_op jit(solution)/shard_map/jit(_take)/gather | solution.py:112
  49.7 15.8 %all-gather.2.cloned.1.call-done = bf16[256,5120]{1,0:T(8,128)(2,1)} async-done(((bf16[256,1280]{1,0:T(8,128)(2,1)}), bf16[256,5120]{1,0:T(8,128)(2,1)}) %all-gather.2.cloned.1.call-update) | async-done | bytes 2621456 | tf_op jit(solution)/shard_map/all_gather | solution.py:70
  65.6 2.3 fusion.35
  67.9 3.1 multiply_reduce_fusion.1
  71.8 3.9 convolution_convert_fusion.1
  76.7 0.8 copy.102
  77.5 4.5 %all-to-all-start.1 = ((bf16[16,2,2,16,128]{4,3,2,1,0:T(8,128)(2,1)}), bf16[16,2,2,16,128]{4,3,2,1,0:T(8,128)(2,1)S(1)}, u32[]{:S(2)}, u32[]{:S(2)}) async-start(bf16[16,2,2,16,128]{4,3,2,1,0:T(8,128)(2,1)} %bitcast.47), calls=%async_computation.1 | async-start | bytes 524288 | tf_op jit(solution)/shard_map/all_to_all | solution.py:105
  82.0 7.5 %broadcast_select_fusion = bf16[32,12,8192]{2,1,0:T(8,128)(2,1)} fusion(bf16[32,12,8192]{2,1,0:T(8,128)(2,1)} %gather.7, pred[32,12]{1,0:T(8,128)(4,1)S(1)} %compare_and_fusion), kind=kLoop, calls=%fused_computation.41 | loop fusion | flops 3145728 | bytes 12583296 | tf_op jit(solution)/shard_map/jit(_take)/select_n | solution.py:112
  89.4 3.8 all-to-all-start
  93.2 0.7 constant_dynamic-slice_fusion.1
  95.6 10.7 %fusion.55 = f32[256,2048]{1,0:T(8,128)S(1)} fusion(bf16[5120,2048]{1,0:T(8,128)(2,1)} %param.16, bf16[256,5120]{1,0:T(8,128)(2,1)} %all-gather.2.cloned.1.call-done, f32[5120]{0:T(1024)S(1)} %copy-done.5, f32[256]{0:T(256)S(1)} %add_rsqrt_fusion.2), kind=kOutput, calls=%fused_computation.111 | convolution fusion | flops 5373952000 | bytes 25711616 | tf_op jit(solution)/shard_map/dot_general | solution.py:75
  107.9 1.9 fusion.38
  109.8 0.8 subtract_convert_fusion
  111.2 163.8 %all-to-all-done = bf16[32,12,8192]{2,1,0:T(8,128)(2,1)} async-done(((bf16[32,12,8192]{2,1,0:T(8,128)(2,1)}), bf16[32,12,8192]{2,1,0:T(8,128)(2,1)}, u32[]{:S(2)}, u32[]{:S(2)}) %all-to-all-start) | async-done | bytes 6291488 | tf_op jit(solution)/shard_map/all_to_all | solution.py:113
  275.1 11.4 %reshape.360 = bf16[32,12,2,2,16,128]{5,4,3,2,1,0:T(8,128)(2,1)} reshape(bf16[32,12,8192]{2,1,0:T(8,128)(2,1)} %all-to-all-done) | data formatting | bytes 12582912 | tf_op jit(solution)/shard_map/reshape | solution.py:115
  286.5 3.9 slice_bitcast_fusion
  290.4 2.6 copy.81
  293.1 2.6 copy.79
  295.7 112.0 %while.13 = (s32[]{:T(128)}, bf16[8,512,128]{2,1,0:T(8,128)(2,1)}, s32[8]{0:T(128)S(1)}, bf16[16,256,128]{2,1,0:T(8,128)(2,1)S(1)}, bf16[2,6144,128]{2,1,0:T(8,1...) while((s32[]{:T(128)}, bf16[8,512,128]{2,1,0:T(8,128)(2,1)}, ...), condition=%wide.region_15.16_spmd.clone, body=%wide.region_10.15_spmd.clone.sunk | while | flops 1713587200 | bytes 43850548 | solution.py:171
  296.9 0.8 fusion.83
  297.9 3.5 fusion.84
  301.8 2.9 fusion.87
  304.7 4.0 fusion.86
  308.7 1.0 fusion.89
  310.9 0.8 fusion.83
  311.9 3.5 fusion.84
  315.8 2.9 fusion.87
  318.7 4.0 fusion.86
  322.7 1.0 fusion.89
  324.9 0.8 fusion.83
  325.9 3.5 fusion.84
  329.8 2.9 fusion.87
  332.7 4.0 fusion.86
  336.7 1.0 fusion.89
  338.9 0.8 fusion.83
  339.9 3.5 fusion.84
  343.8 2.9 fusion.87
  346.7 4.0 fusion.86
  350.7 1.0 fusion.89
  352.9 0.8 fusion.83
  353.9 3.5 fusion.84
  357.8 2.9 fusion.87
  360.7 4.0 fusion.86
  364.7 1.0 fusion.89
  366.9 0.8 fusion.83
  367.9 3.5 fusion.84
  371.8 2.9 fusion.87
  374.7 4.0 fusion.86
  378.7 1.0 fusion.89
  380.9 0.8 fusion.83
  381.9 3.5 fusion.84
  385.8 2.9 fusion.87
  388.7 4.0 fusion.86
  392.7 1.0 fusion.89
  394.9 0.8 fusion.83
  395.9 3.5 fusion.84
  399.8 2.9 fusion.87
  402.7 4.0 fusion.86
  406.7 1.0 fusion.89
  407.7 2.1 copy.86
  409.7 1.2 copy.110
  (125 shorter events, 18.4 us)
Async XLA Ops:
  7.2 60.8 %copy-start = (bf16[5120,256]{1,0:T(8,128)(2,1)S(1)}, bf16[5120,256]{1,0:T(8,128)(2,1)}, u32[]{:S(2)}) copy-start(bf16[5120,256]{1,0:T(8,128)(2,1)} %param.17) | copy-start | bytes 7864324
  7.2 58.4 %all-gather.2.cloned.1.call-start = ((), (), s32[]{:S(2)}) async-start(), calls=%async_computation.2 | async-start | bytes 3276800 | tf_op jit(solution)/shard_map/all_gather | solution.py:70
  40.4 8.6 %copy-start.6 = (s32[1,16,1]{1,2,0:T(1,128)S(1)}, s32[1,16,1]{1,2,0:T(1,128)}, u32[]{:S(2)}) copy-start(s32[1,16,1]{1,2,0:T(1,128)} %param.25) | copy-start | bytes 196
  40.4 27.6 %copy-start.5 = (f32[5120]{0:T(1024)S(1)}, f32[5120]{0:T(1024)}, u32[]{:S(2)}) copy-start(f32[5120]{0:T(1024)} %param.15) | copy-start | bytes 61444
  67.9 3.3 copy-start.3
  77.5 12.0 %all-to-all-start.1 = ((bf16[16,2,2,16,128]{4,3,2,1,0:T(8,128)(2,1)}), bf16[16,2,2,16,128]{4,3,2,1,0:T(8,128)(2,1)S(1)}, u32[]{:S(2)}, u32[]{:S(2)}) async-start(bf16[16,2,2,16,128]{4,3,2,1,0:T(8,128)(2,1)} %bitcast.47), calls=%async_computation.1 | async-start | bytes 524288 | tf_op jit(solution)/shard_map/all_to_all | solution.py:105
  89.4 185.6 %all-to-all-start = ((bf16[32,12,8192]{2,1,0:T(8,128)(2,1)}), bf16[32,12,8192]{2,1,0:T(8,128)(2,1)}, u32[]{:S(2)}, u32[]{:S(2)}) async-start(bf16[32,12,8192]{2,1,0:T(8,128)(2,1)} %broadcast_select_fusion), calls=%async_computation | async-start | bytes 16777216 | tf_op jit(solution)/shard_map/all_to_all | solution.py:113
  106.3 1.4 copy-start.2
  106.3 1.5 copy-start.4
  407.7 4.0 copy-start.1
Sparse Core Ops, SparseCore 0:
  9.6 55.9 all-gather.1
where the time goes:
time: 425 us; the launch traced here: 419 us
  waiting for transfers between devices  180 us (42%)
  matrix products  88.1 us (21%)
  local copies, waits for them, and re-layouts  71.7 us (17%)
  other arithmetic  49.9 us (12%)
  between operations  15 us (4%)
  starting transfers between devices  8.32 us (2%)
  loops' own time  5.16 us (1%)
    all_to_all x1, waiting for transfers between devices, shards(): lax.all_to_all(outgoing, ('dp', 'tensor'), split_axis=0, concat_axis=0, t...  164 us
    dot_general x8, matrix products, pair_block(): jnp.dot(prior_exp.astype(jnp.bfloat16), prior_values, preferred_element_t...  32.2 us
    dot_general x8, matrix products, pair_block(): jnp.einsum('qd,kd->qk', head_rows, prior_keys, preferred_element_type=jnp...  28.3 us
    gather x2, local copies, waits for them, and re-layouts, shards(): outgoing = jnp.take(flat_pool, row_ids.reshape(-1), axis=0)  27 us
    reduce_sum x16, other arithmetic, pair_block(): total = jnp.sum(prior_exp, axis=1) + jnp.sum(recent_exp, axis=1)  23.9 us
    all_gather x1, waiting for transfers between devices, shards(): full_rows = lax.all_gather(hidden, 'tensor', axis=1, tiled=True)  15.8 us
    reshape x1, local copies, waits for them, and re-layouts, shards(): arrived.reshape(sources, capacity, key_heads, 2, PAGE_TOKENS, HEAD_SIZE)  11.4 us
    dot_general x1, matrix products, shards(): jnp.dot(normalized_rows, w_query, preferred_element_type=jnp.float32)  10.7 us
  transfers between devices with their start and end apart: 3, of which 2 were waited for; matrix products, arithmetic and copies ran while one was open for 16% of the time, Pallas kernels for 0%

commit v1 on v0

--- a/solution.py
+++ b/solution.py
@@ -1,8 +1,11 @@
+import functools
 import math
 
 import jax
 import jax.numpy as jnp
 from jax import lax
+from jax.experimental import pallas as pl
+from jax.experimental.pallas import tpu as pltpu
 from jax.sharding import PartitionSpec as P
 
 HEAD_SIZE = 128
@@ -43,6 +46,173 @@
     landed = matches[:, :, None] & (ranks[:, :, None] == places[None, None, :])
     picked = jnp.sum(jnp.where(landed, payload[:, :, None], 0), axis=1)
     return (picked, jnp.any(landed, axis=1))
+
+
+def gather_kernel(key_heads, rows, capacity, picked_ref, pool_ref, *refs):
+    outs, sem = refs[:key_heads], refs[key_heads]
+
+    def send(n, carry):
+        r = n // capacity
+        c = n - r * capacity
+        slot = picked_ref[n]
+        for h in range(key_heads):
+            pltpu.make_async_copy(
+                pool_ref.at[slot, :, h], outs[h].at[r, :, c], sem.at[h]
+            ).start()
+        return carry
+
+    lax.fori_loop(0, rows * capacity, send, 0)
+    for h in range(key_heads):
+        pltpu.make_async_copy(outs[h], outs[h], sem.at[h]).wait()
+
+
+def gather_pages(picked, pool, key_heads):
+    rows, capacity = picked.shape
+    slots, groups = pool.shape[0], pool.shape[1] // key_heads
+    split_pool = pool.reshape((slots, groups, key_heads) + pool.shape[2:])
+    out = jax.ShapeDtypeStruct((rows, groups, capacity) + pool.shape[2:], pool.dtype)
+    return pl.pallas_call(
+        functools.partial(gather_kernel, key_heads, rows, capacity),
+        out_shape=[out] * key_heads,
+        in_specs=[
+            pl.BlockSpec(memory_space=pltpu.SMEM),
+            pl.BlockSpec(memory_space=pl.ANY),
+        ],
+        out_specs=[pl.BlockSpec(memory_space=pl.ANY)] * key_heads,
+        scratch_shapes=[pltpu.SemaphoreType.DMA((key_heads,))],
+        name="gather_pages",
+    )(picked.reshape(-1), split_pool)
+
+
+BLOCK_PAGES = 32
+ROW_TILES = 2
+
+
+def attention_kernel(
+    group, scale, places_ref, length_ref, q_ref, k_ref, v_ref, pages_ref, *refs
+):
+    out_ref, keys, values, acc, top = refs[-5:]
+    length = length_ref[0]
+    columns = BLOCK_PAGES * PAGE_TOKENS
+    live_pages = (length + PAGE_TOKENS - 1) // PAGE_TOKENS
+    full = length // columns
+    blocks = (length + columns - 1) // columns
+    ones = jnp.ones((PAGE_TOKENS, HEAD_SIZE), jnp.bfloat16)
+    factor = scale * math.log2(math.e)
+
+    def place(i, carry):
+        for u in range(8):
+            j = i * 8 + u
+            at = places_ref[j]
+            keys[j] = pages_ref[at, 0]
+            values[j, :, :HEAD_SIZE] = pages_ref[at, 1]
+            values[j, :, HEAD_SIZE:] = ones
+        return carry
+
+    lax.fori_loop(0, (live_pages + 7) // 8, place, 0)
+
+    def spare(j, carry):
+        values[j] = jnp.zeros(values.shape[1:], jnp.bfloat16)
+        keys[j] = jnp.zeros(keys.shape[1:], jnp.bfloat16)
+        return carry
+
+    lax.fori_loop((live_pages + 7) // 8 * 8, blocks * BLOCK_PAGES, spare, 0)
+    rows = q_ref.shape[0]
+    row_ids = lax.broadcasted_iota(jnp.int32, (rows, rows), 0)
+    column_ids = lax.broadcasted_iota(jnp.int32, (rows, rows), 1)
+    causal = row_ids >= column_ids
+    span_keys = k_ref[...]
+    span_values = jnp.concatenate(
+        [v_ref[...], jnp.ones((rows, HEAD_SIZE), jnp.bfloat16)], axis=1
+    )
+    contract_last = (((1,), (1,)), ((), ()))
+
+    def scores_of(query, key_rows):
+        return (
+            lax.dot_general(query, key_rows, contract_last, preferred_element_type=jnp.float32)
+            * factor
+        )
+
+    for g in range(0, group, ROW_TILES):
+        queries = [q_ref[:, (g + t) * HEAD_SIZE : (g + t + 1) * HEAD_SIZE] for t in range(ROW_TILES)]
+        for t in range(ROW_TILES):
+            recent = jnp.where(causal, scores_of(queries[t], span_keys), NEG)
+            peak = jnp.max(recent, axis=1, keepdims=True)
+            weights = jnp.exp2(recent - peak).astype(jnp.bfloat16)
+            top[t] = jnp.broadcast_to(peak, (rows, HEAD_SIZE))
+            acc[t] = jnp.dot(weights, span_values, preferred_element_type=jnp.float32)
+
+        def step(i, masked):
+            start = pl.multiple_of(i * BLOCK_PAGES, BLOCK_PAGES)
+            key_rows = keys[pl.ds(start, BLOCK_PAGES)].reshape(columns, HEAD_SIZE)
+            value_rows = values[pl.ds(start, BLOCK_PAGES)].reshape(columns, 2 * HEAD_SIZE)
+            for t in range(ROW_TILES):
+                scores = scores_of(queries[t], key_rows)
+                if masked:
+                    positions = i * columns + lax.broadcasted_iota(jnp.int32, scores.shape, 1)
+                    scores = jnp.where(positions < length, scores, NEG)
+                before = top[t][:, :1]
+                peak = jnp.maximum(before, jnp.max(scores, axis=1, keepdims=True))
+                weights = jnp.exp2(scores - peak).astype(jnp.bfloat16)
+                acc[t] = acc[t] * jnp.exp2(before - peak) + jnp.dot(
+                    weights, value_rows, preferred_element_type=jnp.float32
+                )
+                top[t] = jnp.broadcast_to(peak, (rows, HEAD_SIZE))
+
+        lax.fori_loop(0, full, lambda i, c: (step(i, False), c)[1], 0)
+
+        @pl.when(full < blocks)
+        def _():
+            step(full, True)
+
+        for t in range(ROW_TILES):
+            mixed = acc[t]
+            out_ref[:, (g + t) * HEAD_SIZE : (g + t + 1) * HEAD_SIZE] = (
+                mixed[:, :HEAD_SIZE] / mixed[:, HEAD_SIZE:]
+            ).astype(jnp.bfloat16)
+
+
+def attend(places, prefix_len, queries, new_keys, new_values, pages, h, key_heads, out, scale):
+    rows, width = queries.shape
+    part = width // key_heads
+    group = part // HEAD_SIZE
+    most = places.shape[0]
+    vmem = lambda block, index: pl.BlockSpec(block, index)
+    in_specs = [
+        pl.BlockSpec(memory_space=pltpu.SMEM),
+        pl.BlockSpec(memory_space=pltpu.SMEM),
+        vmem((rows, part), lambda i: (0, h)),
+        vmem((rows, HEAD_SIZE), lambda i: (0, h)),
+        vmem((rows, HEAD_SIZE), lambda i: (0, h)),
+        vmem(pages.shape, lambda i: (0,) * pages.ndim),
+    ]
+    operands = [places, prefix_len, queries, new_keys, new_values, pages]
+    aliases = {}
+    if out is not None:
+        in_specs.append(pl.BlockSpec(memory_space=pl.ANY))
+        operands.append(out)
+        aliases = {len(operands) - 1: 0}
+    return pl.pallas_call(
+        functools.partial(attention_kernel, group, scale),
+        grid=(1,),
+        out_shape=jax.ShapeDtypeStruct((rows, width), jnp.bfloat16),
+        in_specs=in_specs,
+        out_specs=vmem((rows, part), lambda i: (0, h)),
+        scratch_shapes=[
+            pltpu.VMEM((most, PAGE_TOKENS, HEAD_SIZE), jnp.bfloat16),
+            pltpu.VMEM((most, PAGE_TOKENS, 2 * HEAD_SIZE), jnp.bfloat16),
+            pltpu.VMEM((ROW_TILES, rows, 2 * HEAD_SIZE), jnp.float32),
+            pltpu.VMEM((ROW_TILES, rows, HEAD_SIZE), jnp.float32),
+        ],
+        input_output_aliases=aliases,
+        compiler_params=pltpu.CompilerParams(vmem_limit_bytes=40 * 2**20),
+        cost_estimate=pl.CostEstimate(
+            flops=4 * rows * part * most * PAGE_TOKENS,
+            bytes_accessed=2 * pages.size,
+            transcendentals=rows * group * most * PAGE_TOKENS,
+        ),
+        name="attend_head",
+    )(*operands)
 
 
 def shards(
@@ -106,74 +276,35 @@
     own_row = lax.dynamic_index_in_dim(page_owner, request, 0, keepdims=False)
     my_device = request * tensor_ways + lax.axis_index("tensor")
     picked, unused = collect(page_owner == my_device, page_slot, capacity)
-    group_ids = jnp.arange(tensor_ways, dtype=jnp.int32)
-    row_ids = picked[:, None, :] * tensor_ways + group_ids[None, :, None]
-    flat_pool = kv_pool.reshape(slot_count * tensor_ways, key_heads * 2 * PAGE_TOKENS * HEAD_SIZE)
-    outgoing = jnp.take(flat_pool, row_ids.reshape(-1), axis=0)
-    arrived = lax.all_to_all(outgoing, ("dp", "tensor"), split_axis=0, concat_axis=0, tiled=True)
+    outgoing = gather_pages(picked, kv_pool, key_heads)
     sources = data_ways * tensor_ways
-    received = arrived.reshape(sources, capacity, key_heads, 2, PAGE_TOKENS, HEAD_SIZE)
-    source_match = own_row[None, :] == jnp.arange(sources, dtype=jnp.int32)[:, None]
-    page_numbers = jnp.broadcast_to(
-        jnp.arange(MOST_PAGES, dtype=jnp.int32)[None, :], (sources, MOST_PAGES)
-    )
-    page_of, present = collect(source_match, page_numbers, capacity)
-    token_pos = (
-        page_of[:, :, None] * PAGE_TOKENS + jnp.arange(PAGE_TOKENS, dtype=jnp.int32)[None, None, :]
-    )
-    live = (present[:, :, None] & (token_pos < length)).reshape(sources * capacity * PAGE_TOKENS)
-    stored_key_rows = (
-        received[:, :, :, 0]
-        .transpose(2, 0, 1, 3, 4)
-        .reshape(key_heads, sources * capacity * PAGE_TOKENS, HEAD_SIZE)
-    )
-    stored_value_rows = (
-        received[:, :, :, 1]
-        .transpose(2, 0, 1, 3, 4)
-        .reshape(key_heads, sources * capacity * PAGE_TOKENS, HEAD_SIZE)
-    )
-    heads_per_group = local_heads // key_heads
-    queries_by_head = queries.transpose(1, 0, 2)
-    row_offsets = jnp.arange(2 * SPAN, dtype=jnp.int32) % SPAN
-    causal = row_offsets[:, None] >= offsets[None, :]
-
-    def pair_block(block):
-        head_rows = lax.dynamic_slice_in_dim(queries_by_head, 2 * block, 2, 0).reshape(
-            2 * SPAN, HEAD_SIZE
+    arrived = [
+        lax.all_to_all(
+            pages.reshape((sources, capacity) + pages.shape[3:]),
+            ("dp", "tensor"),
+            split_axis=0,
+            concat_axis=0,
+            tiled=True,
+        ).reshape((sources * capacity,) + pages.shape[3:])
+        for pages in outgoing
+    ]
+    same = own_row[:, None] == own_row[None, :]
+    later = jnp.arange(MOST_PAGES)[:, None] > jnp.arange(MOST_PAGES)[None, :]
+    places = own_row * capacity + jnp.sum(same & later, axis=1).astype(jnp.int32)
+    attn_out = None
+    for h in range(key_heads):
+        attn_out = attend(
+            places,
+            prefix_len,
+            queries.reshape(SPAN, local_heads * HEAD_SIZE),
+            new_keys.reshape(SPAN, key_heads * HEAD_SIZE),
+            fresh_value_rows.reshape(SPAN, key_heads * HEAD_SIZE),
+            arrived[h],
+            h,
+            key_heads,
+            attn_out,
+            scale,
         )
-        kv_index = 2 * block // heads_per_group
-        prior_keys = lax.dynamic_index_in_dim(stored_key_rows, kv_index, 0, keepdims=False)
-        prior_values = lax.dynamic_index_in_dim(stored_value_rows, kv_index, 0, keepdims=False)
-        span_keys = lax.dynamic_index_in_dim(new_keys, kv_index, 1, keepdims=False)
-        span_values = lax.dynamic_index_in_dim(fresh_value_rows, kv_index, 1, keepdims=False)
-        prior = (
-            jnp.einsum("qd,kd->qk", head_rows, prior_keys, preferred_element_type=jnp.float32)
-            * scale
-        )
-        prior = jnp.where(live[None, :], prior, NEG)
-        recent = (
-            jnp.einsum("qd,kd->qk", head_rows, span_keys, preferred_element_type=jnp.float32)
-            * scale
-        )
-        recent = jnp.where(causal, recent, NEG)
-        peak = jnp.maximum(jnp.max(prior, axis=1), jnp.max(recent, axis=1))[:, None]
-        prior_exp = jnp.exp(prior - peak)
-        recent_exp = jnp.exp(recent - peak)
-        total = jnp.sum(prior_exp, axis=1) + jnp.sum(recent_exp, axis=1)
-        mixed = jnp.dot(
-            prior_exp.astype(jnp.bfloat16), prior_values, preferred_element_type=jnp.float32
-        )
-        mixed = mixed + jnp.dot(
-            recent_exp.astype(jnp.bfloat16), span_values, preferred_element_type=jnp.float32
-        )
-        return (mixed / total[:, None]).astype(jnp.bfloat16)
-
-    blocks = lax.map(pair_block, jnp.arange(local_heads // 2, dtype=jnp.int32))
-    attn_out = (
-        blocks.reshape(local_heads, SPAN, HEAD_SIZE)
-        .transpose(1, 0, 2)
-        .reshape(SPAN, local_heads * HEAD_SIZE)
-    )
     return (attn_out, fresh_page_store)
 
 

time: 425 us -> 471 us (1.11)
  the two profiles are of different devices: /device:TPU:7 before, /device:TPU:13 now
where the time goes in v1:
time: 471 us; the launch traced here: 470 us
  Pallas kernels  261 us (55%)
  blocking collectives  75.5 us (16%)
  waiting for transfers between devices  64.2 us (14%)
  matrix products  17.4 us (4%)
  between operations  15 us (3%)
  other arithmetic  14.4 us (3%)
  local copies, waits for them, and re-layouts  13 us (3%)
  starting transfers between devices  9.32 us (2%)
    pallas_call x1, Pallas kernels, gather_pages(): pl.pallas_call(functools.partial(gather_kernel, key_heads, rows, capacity...  192 us
    all_to_all x1, blocking collectives, shards(): lax.all_to_all(pages.reshape((sources, capacity) + pages.shape[3:]), ('dp...  75.5 us
    pallas_call x2, Pallas kernels, attend(): pl.pallas_call(functools.partial(attention_kernel, group, scale), grid=(1...  68.8 us
    all_gather x1, waiting for transfers between devices, shards(): full_rows = lax.all_gather(hidden, 'tensor', axis=1, tiled=True)  50.6 us
    all_to_all x1, waiting for transfers between devices, shards(): lax.all_to_all(pages.reshape((sources, capacity) + pages.shape[3:]), ('dp...  12.9 us
    dot_general x1, matrix products, shards(): jnp.dot(normalized_rows, w_query, preferred_element_type=jnp.float32)  10.7 us
  transfers between devices with their start and end apart: 3, of which 2 were waited for; matrix products, arithmetic and copies ran while one was open for 6% of the time, Pallas kernels for 48%

profile of v1, /device:TPU:13, one launch (start us, length us, event | category | flops | bytes accessed | tf_op | source)
XLA Modules:
  0.0 470.0 jit_solution(17889926342995372130)
XLA Ops:
  7.2 0.0 copy-start
  7.2 0.0 copy-start.10
  7.2 0.0 all-gather.2.cloned.1.call-start
  7.2 0.7 all-gather.2.cloned.1.call-update
  8.6 0.7 convert_bitcast_fusion
  9.3 0.6 reduce-window.6
  9.9 0.2 slice_reduce_fusion
  10.1 0.6 slice.23
  10.8 0.9 convert_reduce_fusion.1
  11.7 0.7 multiply_add_fusion.1
  12.3 0.5 multiply_cosine_fusion
  12.9 50.6 %all-gather.2.cloned.1.call-done = bf16[256,5120]{1,0:T(8,128)(2,1)} async-done(((bf16[256,1280]{1,0:T(8,128)(2,1)}), bf16[256,5120]{1,0:T(8,128)(2,1)}) %all-gather.2.cloned.1.call-update) | async-done | bytes 2621456 | tf_op jit(solution)/shard_map/all_gather | solution.py:240
  63.5 0.0 copy-start.5
  63.5 2.5 fusion
  66.0 0.0 copy-done.10
  66.0 0.0 copy-done.5
  66.0 0.0 copy-start.6
  66.1 2.7 convolution_convert_fusion.1.v_ref
  68.8 0.0 copy-done.6
  68.8 0.0 copy-done
  68.8 0.0 copy-start.8
  68.9 3.8 multiply_reduce_fusion.1
  72.7 1.1 copy.35
  73.8 0.0 copy-done.8
  73.8 0.1 multiply_multiply_fusion.1
  73.9 0.2 subtract_convert_fusion.1
  74.1 0.1 maximum_bitcast_fusion
  74.2 0.3 fusion.3
  74.5 0.8 copy.44
  75.2 4.7 %all-to-all-start.2 = ((bf16[16,2,2,16,128]{4,3,2,1,0:T(8,128)(2,1)}), bf16[16,2,2,16,128]{4,3,2,1,0:T(8,128)(2,1)S(1)}, u32[]{:S(2)}, u32[]{:S(2)}) async-start(bf16[16,2,2,16,128]{4,3,2,1,0:T(8,128)(2,1)} %bitcast.56), calls=%async_computation.2 | async-start | bytes 524288 | tf_op jit(solution)/shard_map/all_to_all | solution.py:275
  80.0 0.8 add_bitcast_fusion
  80.7 1.0 select_reduce_fusion
  81.7 0.1 copy.37
  81.8 0.6 reshape.206.picked_ref
  82.4 192.4 %gather_pages.1 = (bf16[8,4,12,2,16,128]{5,4,3,2,1,0:T(8,128)(2,1)}, bf16[8,4,12,2,16,128]{5,4,3,2,1,0:T(8,128)(2,1)}) custom-call(s32[96]{0:T(128)} %reshape.206.picked_ref, bf16[96,4,2,2,16,128]{5,4,3,2,1,0:T(8,128)(2,1)} %bitcast.49), custom_call_target="tpu_custom_call" | custom-call | tf_op jit(solution)/shard_map/gather_pages/pallas_call | solution.py:74
  274.8 0.0 all-to-all-done.2
  274.8 75.5 %all_to_all.15 = bf16[32,12,2,16,128]{4,3,2,1,0:T(8,128)(2,1)} all-to-all(bf16[32,12,2,16,128]{4,3,2,1,0:T(8,128)(2,1)} %bitcast.52), channel_id=1, replica_groups=mesh['dp'=8,'tensor'=4] {'dp','tensor'}, dimensions={0} | all-to-all | bytes 6291456 | tf_op jit(solution)/shard_map/all_to_all | solution.py:282
  350.3 4.5 all-to-all-start
  354.9 0.7 constant_dynamic-slice_fusion
  355.6 0.2 convert_reduce_fusion
  355.8 0.0 copy-done.7
  355.8 10.7 %convolution_bitcast_fusion = f32[32,8,16,128]{3,1,2,0:T(8,128)S(1)} fusion(bf16[5120,2048]{1,0:T(8,128)(2,1)} %param.14, bf16[256,5120]{1,0:T(8,128)(2,1)} %all-gather.2.cloned.1.call-done, f32[5120]{0:T(1024)} %param.13, f32[256]{0:T(256)S(1)} %copy-done.7), kind=kOutput, calls=%fused_computation.10 | convolution fusion | flops 5373952000 | bytes 25711616 | tf_op jit(solution)/shard_map/dot_general | solution.py:245
  366.5 0.0 copy-start.9
  366.5 0.4 copy.41
  366.9 0.0 copy-start.4
  366.9 1.3 copy-done.4
  368.2 1.3 multiply_reduce_fusion
  369.4 1.6 copy.33
  371.0 1.3 add_rsqrt_fusion
  372.4 1.5 copy.34
  373.8 0.0 copy-done.9
  373.8 2.0 multiply_multiply_fusion
  375.8 0.9 subtract_convert_fusion
  376.7 0.0 copy-start.1
  376.7 0.6 pad_maximum_fusion
  377.3 0.3 copy.51
  377.6 0.1 copy_bitcast_fusion.1.k_ref
  377.7 0.9 copy-done.1
  378.6 33.7 %attend_head.2.refs_0_ = bf16[256,2048]{1,0:T(8,128)(2,1)} custom-call(s32[256]{0:T(256)S(1)} %multiply_add_fusion.places_ref, s32[1]{0:T(128)} %copy.54.length_ref, bf16[256,2048]{1,0:T(8,128)(2,1)S(1)} %bitcast.46, bf16[256,256]{1,0:T(8,128)(2,1)S(1)} %copy_bitcast_fusion.1.k_ref, bf16[256,256]{1,0:T(8,128)(2,1)S(1)} %convolution_convert_fusion.1.v_ref, ...), custom_call_target="tpu_custom_call" | custom-call | flops 4294967296 | bytes 3145728 | tf_op jit(solution)/shard_map/attend_head/pallas_call | solution.py:195
  412.3 1.0 copy-done.2
  413.3 12.9 %all-to-all-done = bf16[32,12,2,16,128]{4,3,2,1,0:T(8,128)(2,1)} async-done(((bf16[32,12,2,16,128]{4,3,2,1,0:T(8,128)(2,1)}), bf16[32,12,2,16,128]{4,3,2,1,0:T(8,128)(2,1)}, u32[]{:S(2)}, u32[]{:S(2)}) %all-to-all-start) | async-done | bytes 3145760 | tf_op jit(solution)/shard_map/all_to_all | solution.py:282
  426.2 1.2 copy-done.3
  427.4 35.1 %attend_head.3 = bf16[256,2048]{1,0:T(8,128)(2,1)} custom-call(s32[256]{0:T(256)S(1)} %multiply_add_fusion.places_ref, s32[1]{0:T(128)} %copy.54.length_ref, bf16[256,2048]{1,0:T(8,128)(2,1)S(1)} %bitcast.47, bf16[256,256]{1,0:T(8,128)(2,1)S(1)} %copy_bitcast_fusion.1.k_ref, ...), custom_call_target="tpu_custom_call", output_to_operand_aliasing={{}: (6, {})} | custom-call | flops 4294967296 | bytes 3145728 | tf_op jit(solution)/shard_map/attend_head/pallas_call | solution.py:195
  462.5 0.7 copy.55
  (12 shorter events, 0.2 us)
Async XLA Ops:
  7.2 61.7 %copy-start = (bf16[5120,256]{1,0:T(8,128)(2,1)S(1)}, bf16[5120,256]{1,0:T(8,128)(2,1)}, u32[]{:S(2)}) copy-start(bf16[5120,256]{1,0:T(8,128)(2,1)} %param.15) | copy-start | bytes 7864324
  7.2 58.8 %copy-start.10 = (f32[5120]{0:T(1024)S(1)}, f32[5120]{0:T(1024)}, u32[]{:S(2)}) copy-start(f32[5120]{0:T(1024)} %param.13) | copy-start | bytes 61444
  7.2 56.3 %all-gather.2.cloned.1.call-start = ((), (), s32[]{:S(2)}) async-start(), calls=%async_computation.3 | async-start | bytes 3276800 | tf_op jit(solution)/shard_map/all_gather | solution.py:240
  63.5 2.5 copy-start.5
  66.0 2.8 copy-start.6
  68.8 4.9 %copy-start.8 = (f32[128]{0:T(128)S(1)}, f32[128]{0:T(128)}, u32[]{:S(2)}) copy-start(f32[128]{0:T(128)} %param.18) | copy-start | bytes 1540
  75.2 199.5 %all-to-all-start.2 = ((bf16[16,2,2,16,128]{4,3,2,1,0:T(8,128)(2,1)}), bf16[16,2,2,16,128]{4,3,2,1,0:T(8,128)(2,1)S(1)}, u32[]{:S(2)}, u32[]{:S(2)}) async-start(bf16[16,2,2,16,128]{4,3,2,1,0:T(8,128)(2,1)} %bitcast.56), calls=%async_computation.2 | async-start | bytes 524288 | tf_op jit(solution)/shard_map/all_to_all | solution.py:275
  350.3 5.5 %copy-start.7 = (f32[256]{0:T(256)S(1)}, f32[256]{0:T(256)}, u32[]{:S(2)}) copy-start(f32[256]{0:T(256)} %copy-done.6) | copy-start | bytes 3076
  350.3 75.8 %all-to-all-start = ((bf16[32,12,2,16,128]{4,3,2,1,0:T(8,128)(2,1)}), bf16[32,12,2,16,128]{4,3,2,1,0:T(8,128)(2,1)}, u32[]{:S(2)}, u32[]{:S(2)}) async-start(bf16[32,12,2,16,128]{4,3,2,1,0:T(8,128)(2,1)} %bitcast.51), calls=%async_computation | async-start | bytes 6291456 | tf_op jit(solution)/shard_map/all_to_all | solution.py:282
  366.5 7.4 %copy-start.9 = (f32[128]{0:T(128)S(1)}, f32[128]{0:T(128)}, u32[]{:S(2)}) copy-start(f32[128]{0:T(128)} %param.17) | copy-start | bytes 1540
  366.9 1.3 copy-start.4
  376.7 1.9 copy-start.1
  412.3 1.0 copy-start.2
  426.2 1.2 copy-start.3
Sparse Core Ops, SparseCore 0:
  9.6 53.8 all-gather.1
